TPU v7x, 32 devices: a whole 2x2x4 slice. The times are simulated.
32 devices in a mesh: grp: 2 (over x), row: 16 (over z, y, core).
Axes of the slice: x: 2, y: 2, z: 4, core: 2. Of those that a mesh axis runs over, the one named last changes fastest.
Arguments:
- inputs: bfloat16 [8192, 8192], P(('grp', 'row')), parts along dimension 0, may hold values from -6 to 6
- out_grads: bfloat16 [8192, 8192], P(('grp', 'row')), parts along dimension 0, may hold values from -6 to 6
- proj_in: bfloat16 [8192, 64], replicated, may hold values from -0.0625 to 0.0625
- proj_out: bfloat16 [8192, 64], replicated, may hold values from -0.0625 to 0.0625
- example_ids: int32 [8192], P(('grp', 'row')), parts along dimension 0, may hold values from 0 to 7, as said below
Outputs:
- gram: float32 [256, 128], P(('grp', 'row')), parts along dimension 0
There are 2 independent parts, one for each index of `grp`. A program takes and returns all parts, laid end to end along the dimension named above; an argument that names none is the same for every part. Nothing has to cross between parts.
Inputs may be any that keep to these rules, and one draw needn't show every extreme that they name: `example_ids`: within each aligned block of 256 tokens every value 0 to 7 appears exactly 32 times, in an order drawn from the seed.
All inputs are finite; a program needn't handle non-finite values.
Results may differ from a plain program's by a relative error of at most 0.0025.
Values may be sent and summed in bfloat16 or wider, within the bound.
A program may use at most 64 MiB of HBM per device.

v0:
```python
import math

import jax
import jax.numpy as jnp
from jax import lax
from jax.sharding import PartitionSpec as P

RANK = 64
TPE = 32
EX_DEV = 8


def tile_of(mine, other):
    product = lax.dot_general(
        mine, other, (((1,), (1,)), ((), ())), preferred_element_type=jnp.float32
    )
    return product / RANK


def shards(inputs, out_grads, proj_in, proj_out, example_ids):
    xproj = jnp.dot(inputs, proj_in, preferred_element_type=jnp.float32).astype(jnp.bfloat16)
    gproj = jnp.dot(out_grads, proj_out, preferred_element_type=jnp.float32).astype(jnp.bfloat16)
    onehot = (example_ids[None, :] == jnp.arange(EX_DEV, dtype=jnp.int32)[:, None]).astype(
        jnp.bfloat16
    )
    weighted = onehot[:, :, None] * gproj[None, :, :]
    outer = jnp.einsum("etp,tq->epq", weighted, xproj, preferred_element_type=jnp.float32)
    scale_factor = 1.0 / math.sqrt(TPE)
    features = (outer.reshape(EX_DEV, RANK * RANK) * scale_factor).astype(jnp.bfloat16)
    return tile_of(features, lax.all_gather(features, "row", axis=0, tiled=True))


def solution(mesh):
    in_specs = (P(("grp", "row"), None), P(("grp", "row"), None), P(), P(), P(("grp", "row")))
    out_specs = P(("grp", "row"), None)
    return jax.shard_map(shards, mesh=mesh, in_specs=in_specs, out_specs=out_specs, check_vma=False)
```

profile of v0, /device:TPU:0, one launch (start us, length us, event | category | flops | bytes accessed | tf_op | source)
XLA Modules:
  0.0 65.8 jit_solution(11964064832021179859)
XLA Ops:
  6.5 0.0 copy-start
  6.5 0.0 all-gather.2.cloned.1.call-start
  6.5 0.8 %fusion.5 = bf16[8,256]{1,0:T(8,128)(2,1)S(1)} fusion(s32[256]{0:T(256)} %param.9), kind=kLoop, calls=%fused_computation.10 | loop fusion | flops 4096 | bytes 5120 | tf_op jit(solution)/shard_map/convert_element_type | solution.py:23
  7.3 3.9 %convolution_convert_fusion.1 = bf16[256,64]{0,1:T(8,128)(2,1)S(1)} fusion(bf16[256,8192]{1,0:T(8,128)(2,1)} %param.6, bf16[8192,64]{0,1:T(8,128)(2,1)} %param.8), kind=kOutput, calls=%fused_computation.3 | convolution fusion | flops 268451840 | bytes 5275648 | tf_op jit(solution)/shard_map/dot_general | solution.py:22
  11.2 0.0 copy-done
  11.2 3.9 %fusion = bf16[8,64,64]{2,1,0:T(8,128)(2,1)S(1)} fusion(bf16[256,8192]{1,0:T(8,128)(2,1)} %param.5, bf16[8192,64]{0,1:T(8,128)(2,1)S(1)} %copy-done, bf16[256,64]{0,1:T(8,128)(2,1)S(1)} %convolution_convert_fusion.1, bf16[8,256]{1,0:T(8,128)(2,1)S(1)} %fusion.5), kind=kOutput, calls=%fused_computation.1 | convolution fusion | flops 285425664 | bytes 5345280 | tf_op jit(solution)/shard_map/etp,tq->epq/dot_general | solution.py:27
  15.1 0.8 %convert_element_type.23 = bf16[8,4096]{1,0:T(8,128)(2,1)} reshape(bf16[8,64,64]{2,1,0:T(8,128)(2,1)S(1)} %fusion) | data formatting | bytes 131072 | tf_op jit(solution)/shard_map/convert_element_type | solution.py:29
  15.9 0.0 all-gather.2.cloned.1.call-update
  15.9 40.8 %all-gather.2.cloned.1.call-done = bf16[128,4096]{1,0:T(8,128)(2,1)} async-done(((bf16[8,4096]{1,0:T(8,128)(2,1)}), bf16[128,4096]{1,0:T(8,128)(2,1)}) %all-gather.2.cloned.1.call-update) | async-done | bytes 1048592 | tf_op jit(solution)/shard_map/all_gather | solution.py:30
  56.7 2.2 %convolution_multiply_fusion.1 = f32[8,128]{1,0:T(8,128)} fusion(bf16[8,4096]{1,0:T(8,128)(2,1)} %convert_element_type.23, bf16[128,4096]{1,0:T(8,128)(2,1)} %all-gather.2.cloned.1.call-done), kind=kOutput, calls=%fused_computation.5 | convolution fusion | flops 8389632 | bytes 1118208 | tf_op jit(solution)/shard_map/dot_general | solution.py:14
Async XLA Ops:
  6.5 4.7 %copy-start = (bf16[8192,64]{0,1:T(8,128)(2,1)S(1)}, bf16[8192,64]{0,1:T(8,128)(2,1)}, u32[]{:S(2)}) copy-start(bf16[8192,64]{0,1:T(8,128)(2,1)} %param.7) | copy-start | bytes 3145732
  6.5 50.2 %all-gather.2.cloned.1.call-start = ((), (), s32[]{:S(2)}) async-start(), calls=%async_computation | async-start | bytes 1114112 | tf_op jit(solution)/shard_map/all_gather | solution.py:30
Sparse Core Ops, SparseCore 0:
  16.0 40.6 all-gather.1
where the time goes:
time: 66 us; the launch traced here: 65.8 us
  waiting for transfers between devices  40.8 us (62%)
  between operations  13.4 us (20%)
  matrix products  10 us (15%)
  local copies, waits for them, and re-layouts  0.8 us (1%)
  other arithmetic  0.77 us (1%)
    all_gather x1, waiting for transfers between devices, shards(): lax.all_gather(features, 'row', axis=0, tiled=True)  40.8 us
    dot_general x1, matrix products, shards(): jnp.einsum('etp,tq->epq', weighted, xproj, preferred_element_type=jnp.flo...  3.9 us
    dot_general x1, matrix products, shards(): jnp.dot(out_grads, proj_out, preferred_element_type=jnp.float32)  3.88 us
    dot_general x1, matrix products, tile_of(): lax.dot_general(mine, other, (((1,), (1,)), ((), ())), preferred_element_...  2.24 us
  transfers between devices with their start and end apart: 1, of which 1 were waited for; matrix products, arithmetic and copies ran while one was open for 0% of the time, Pallas kernels for 0%

commit v1 on v0

v1 whole, which is shorter than its diff:
```python
import functools
import math

import jax
import jax.numpy as jnp
from jax import lax
from jax.experimental import pallas as pl
from jax.experimental.pallas import tpu as pltpu
from jax.sharding import PartitionSpec as P

RANK = 64
TPE = 32
EX_DEV = 8
LANES = 128
SLICES = 16
CHUNK = 1024
MESH = pl.DeviceIdType.MESH
NT = (((1,), (1,)), ((), ()))


def dot_nt(a, b):
    return lax.dot_general(a, b, NT, preferred_element_type=jnp.float32)


def kernel(
    n,
    x_hbm,
    g_hbm,
    pi_hbm,
    po_hbm,
    ids_hbm,
    out_ref,
    x_buf,
    g_buf,
    pi_buf,
    po_buf,
    ids_ref,
    feat,
    recv,
    gram,
    parts,
    load_sem,
    ids_sem,
    send_a,
    recv_a,
    send_b,
    recv_b,
):
    me = lax.axis_index("row")
    quarter, mine = me // SLICES, me % SLICES
    chunks = x_buf.shape[1] // CHUNK

    loads = []
    for c in range(chunks):
        cols = pl.ds(c * CHUNK, CHUNK)
        pairs = ((pi_hbm, pi_buf), (x_hbm, x_buf), (po_hbm, po_buf), (g_hbm, g_buf))
        loads.append(
            [
                pltpu.make_async_copy(src.at[:, cols], dst.at[:, cols], load_sem.at[c, i])
                for i, (src, dst) in enumerate(pairs)
            ]
        )
        for copy in loads[-1]:
            copy.start()

    ids_copy = pltpu.make_async_copy(ids_hbm, ids_ref, ids_sem)
    ids_copy.start()

    barrier = pltpu.get_barrier_semaphore()
    for d in range(1, n):
        pl.semaphore_signal(
            barrier, inc=1, device_id={"row": lax.rem(me + d, n)}, device_id_type=MESH
        )

    tokens = x_buf.shape[0]
    x = jnp.zeros((tokens, 2 * RANK), jnp.float32)
    g = jnp.zeros((tokens, 2 * RANK), jnp.float32)
    for c in range(chunks):
        cols = pl.ds(c * CHUNK, CHUNK)
        loads[c][0].wait()
        loads[c][1].wait()
        pi = pi_buf[:, cols]
        x += dot_nt(x_buf[:, cols], jnp.concatenate([pi, pi], axis=0))
        loads[c][2].wait()
        loads[c][3].wait()
        po = po_buf[:, cols]
        g += dot_nt(g_buf[:, cols], jnp.concatenate([po, po], axis=0))

    x = x.astype(jnp.bfloat16)
    g = g.astype(jnp.bfloat16).astype(jnp.float32).T[:RANK]
    ids_copy.wait()
    ids = ids_ref[...].reshape(1, tokens)
    onehot = (ids == lax.broadcasted_iota(jnp.int32, (EX_DEV, tokens), 0)).astype(jnp.float32)
    weighted = (g[:, None, :] * onehot[None, :, :]).reshape(RANK * EX_DEV, tokens)
    outer = jnp.dot(weighted.astype(jnp.bfloat16), x, preferred_element_type=jnp.float32)
    half = RANK * EX_DEV // 2
    low = lax.broadcasted_iota(jnp.int32, (half, LANES), 1) < RANK
    packed = jnp.where(low, outer[:half], outer[half:]) * (1.0 / math.sqrt(TPE))
    feat[...] = packed.astype(jnp.bfloat16).reshape(feat.shape)

    pl.semaphore_wait(barrier, n - 1)
    for d in range(1, n):
        target = lax.rem(me + d, n)
        pltpu.make_async_remote_copy(
            src_ref=feat.at[lax.rem(target, SLICES)],
            dst_ref=recv.at[me],
            send_sem=send_a,
            recv_sem=recv_a,
            device_id={"row": target},
            device_id_type=MESH,
        ).start()
    recv[me] = feat[mine]
    rest = recv.at[pl.ds(0, n - 1)]
    pltpu.make_async_copy(rest, rest, recv_a).wait()

    def rows(block):
        block = block.astype(jnp.float32).reshape(-1, 2, EX_DEV, LANES)
        sides = [block[:, i].reshape(-1, LANES) for i in range(2)]
        return jnp.concatenate(sides, axis=1).astype(jnp.bfloat16)

    every = rows(recv[...])
    own = every if n == SLICES else rows(recv[pl.ds(quarter * SLICES, SLICES)])
    gram[...] = dot_nt(own, every).reshape(gram.shape)

    for d in range(1, SLICES):
        to = lax.rem(mine + d, SLICES)
        pltpu.make_async_remote_copy(
            src_ref=gram.at[to],
            dst_ref=parts.at[mine],
            send_sem=send_b,
            recv_sem=recv_b,
            device_id={"row": quarter * SLICES + to},
            device_id_type=MESH,
        ).start()
    parts[mine] = gram[mine]
    rest_b = parts.at[pl.ds(0, SLICES - 1)]
    pltpu.make_async_copy(rest_b, rest_b, recv_b).wait()
    out_ref[...] = jnp.sum(parts[...], axis=0) * (1.0 / RANK)
    pltpu.make_async_copy(rest, rest, send_a).wait()
    pltpu.make_async_copy(rest_b, rest_b, send_b).wait()


def shards(n, inputs, out_grads, proj_in, proj_out, example_ids):
    tokens, width = inputs.shape
    examples = EX_DEV * n
    hbm = pl.BlockSpec(memory_space=pl.ANY)
    vmem = pl.BlockSpec(memory_space=pltpu.VMEM)
    flops = 4 * tokens * width * RANK
    return pl.pallas_call(
        functools.partial(kernel, n),
        out_shape=jax.ShapeDtypeStruct((EX_DEV, examples), jnp.float32),
        in_specs=[hbm] * 5,
        out_specs=vmem,
        scratch_shapes=[
            pltpu.VMEM((tokens, width), jnp.bfloat16),
            pltpu.VMEM((tokens, width), jnp.bfloat16),
            pltpu.VMEM((RANK, width), jnp.bfloat16),
            pltpu.VMEM((RANK, width), jnp.bfloat16),
            pltpu.VMEM((tokens,), jnp.int32),
            pltpu.VMEM((SLICES, 2 * EX_DEV, LANES), jnp.bfloat16),
            pltpu.VMEM((n, 2 * EX_DEV, LANES), jnp.bfloat16),
            pltpu.VMEM((SLICES, EX_DEV, examples), jnp.float32),
            pltpu.VMEM((SLICES, EX_DEV, examples), jnp.float32),
            pltpu.SemaphoreType.DMA((width // CHUNK, 4)),
            pltpu.SemaphoreType.DMA,
            pltpu.SemaphoreType.DMA,
            pltpu.SemaphoreType.DMA,
            pltpu.SemaphoreType.DMA,
            pltpu.SemaphoreType.DMA,
        ],
        compiler_params=pltpu.CompilerParams(
            collective_id=0, has_side_effects=True, vmem_limit_bytes=63 * 1024 * 1024
        ),
        cost_estimate=pl.CostEstimate(
            flops=flops, bytes_accessed=4 * (tokens + RANK) * width, transcendentals=0
        ),
    )(inputs, out_grads, proj_in.T, proj_out.T, example_ids)


def solution(mesh):
    in_specs = (P(("grp", "row"), None), P(("grp", "row"), None), P(), P(), P(("grp", "row")))
    out_specs = P(("grp", "row"), None)
    body = functools.partial(shards, mesh.shape["row"])
    return jax.shard_map(body, mesh=mesh, in_specs=in_specs, out_specs=out_specs, check_vma=False)
```

time: 66 us -> 20 us (0.30)
  waiting for transfers between devices: 40.8 us -> 0 us
  Pallas kernels: 0 us -> 18.5 us
  between operations: 13.4 us -> 0.01 us
  matrix products: 10 us -> 0 us
  other arithmetic: 0.77 us -> 0 us
    all_gather x1 -> x0, waiting for transfers between devices: 40.8 us -> none  [shards(): lax.all_gather(features, 'row', axis=0, tiled=True)]
    pallas_call x0 -> x1, Pallas kernels: none -> 18.5 us  [shards(): pl.pallas_call(functools.partial(kernel, n), out_shape=jax.ShapeDtypeStru...]
    dot_general x3 -> x0, matrix products: 10 us -> none  [the longest x1 3.9 us: shards(): jnp.einsum('etp,tq->epq', weighted, xproj, preferred_element_type=jnp.flo...]
    unnamed x2 -> x1, local copies, waits for them, and re-layouts: 0.01 us -> 1.28 us
    convert_element_type x1 -> x0, local copies, waits for them, and re-layouts: 0.79 us -> none  [shards(): (outer.reshape(EX_DEV, RANK * RANK) * scale_factor).astype(jnp.bfloat16)]
    convert_element_type x1 -> x0, other arithmetic: 0.77 us -> none  [shards(): (example_ids[None, :] == jnp.arange(EX_DEV, dtype=jnp.int32)[:, None]).as...]
  transfers between devices with their start and end apart: 1 -> 0, of which waited for: 1 -> 0; matrix products, arithmetic and copies ran while one was open for 0% -> 0% of each run, Pallas kernels for 0% -> 0%
where the time goes in v1:
time: 20 us; the launch traced here: 19.8 us
  Pallas kernels  18.5 us (92%)
  local copies, waits for them, and re-layouts  1.28 us (6%)
    pallas_call x1, Pallas kernels, shards(): pl.pallas_call(functools.partial(kernel, n), out_shape=jax.ShapeDtypeStru...  18.5 us
    unnamed x1, local copies, waits for them, and re-layouts  1.28 us

profile of v1, /device:TPU:0, one launch (start us, length us, event | category | flops | bytes accessed | tf_op | source)
XLA Modules:
  0.0 19.8 jit_solution(5503182022341145801)
XLA Ops:
  0.0 18.5 %shard_map.55 = f32[8,128]{1,0:T(8,128)} custom-call(bf16[256,8192]{1,0:T(8,128)(2,1)} %x_hbm.1, bf16[256,8192]{1,0:T(8,128)(2,1)} %g_hbm.1, bf16[64,8192]{1,0:T(8,128)(2,1)} %bitcast.2, bf16[64,8192]{1,0:T(8,128)(2,1)} %bitcast.3, s32[256]{0:T(256)} %ids_hbm.1), custom_call_target="tpu_custom_call" | custom-call | flops 536870912 | bytes 10485760 | tf_op jit(solution)/shard_map/pallas_call | solution.py:149
  18.5 1.3 %copy.7 = f32[8,128]{1,0:T(8,128)} copy(f32[8,128]{1,0:T(8,128)} %shard_map.55) | data formatting | bytes 8192

commit v2 on v1

--- a/solution.py
+++ b/solution.py
@@ -35,6 +35,8 @@
     pi_buf,
     po_buf,
     ids_ref,
+    x_sum,
+    g_sum,
     feat,
     recv,
     gram,
@@ -50,17 +52,18 @@
     quarter, mine = me // SLICES, me % SLICES
     chunks = x_buf.shape[1] // CHUNK
 
-    loads = []
-    for c in range(chunks):
-        cols = pl.ds(c * CHUNK, CHUNK)
-        pairs = ((pi_hbm, pi_buf), (x_hbm, x_buf), (po_hbm, po_buf), (g_hbm, g_buf))
-        loads.append(
-            [
-                pltpu.make_async_copy(src.at[:, cols], dst.at[:, cols], load_sem.at[c, i])
-                for i, (src, dst) in enumerate(pairs)
-            ]
-        )
-        for copy in loads[-1]:
+    pairs = ((pi_hbm, pi_buf), (x_hbm, x_buf), (po_hbm, po_buf), (g_hbm, g_buf))
+
+    def loads(c):
+        cols = pl.ds(pl.multiple_of(c * CHUNK, CHUNK), CHUNK)
+        return cols, [
+            pltpu.make_async_copy(src.at[:, cols], dst.at[:, cols], load_sem.at[c, i])
+            for i, (src, dst) in enumerate(pairs)
+        ]
+
+    @pl.loop(0, chunks)
+    def _(c):
+        for copy in loads(c)[1]:
             copy.start()
 
     ids_copy = pltpu.make_async_copy(ids_hbm, ids_ref, ids_sem)
@@ -73,21 +76,23 @@
         )
 
     tokens = x_buf.shape[0]
-    x = jnp.zeros((tokens, 2 * RANK), jnp.float32)
-    g = jnp.zeros((tokens, 2 * RANK), jnp.float32)
-    for c in range(chunks):
-        cols = pl.ds(c * CHUNK, CHUNK)
-        loads[c][0].wait()
-        loads[c][1].wait()
+    x_sum[...] = jnp.zeros_like(x_sum)
+    g_sum[...] = jnp.zeros_like(g_sum)
+
+    @pl.loop(0, chunks)
+    def _(c):
+        cols, copies = loads(c)
+        copies[0].wait()
+        copies[1].wait()
         pi = pi_buf[:, cols]
-        x += dot_nt(x_buf[:, cols], jnp.concatenate([pi, pi], axis=0))
-        loads[c][2].wait()
-        loads[c][3].wait()
+        x_sum[...] += dot_nt(x_buf[:, cols], jnp.concatenate([pi, pi], axis=0))
+        copies[2].wait()
+        copies[3].wait()
         po = po_buf[:, cols]
-        g += dot_nt(g_buf[:, cols], jnp.concatenate([po, po], axis=0))
+        g_sum[...] += dot_nt(g_buf[:, cols], jnp.concatenate([po, po], axis=0))
 
-    x = x.astype(jnp.bfloat16)
-    g = g.astype(jnp.bfloat16).astype(jnp.float32).T[:RANK]
+    x = x_sum[...].astype(jnp.bfloat16)
+    g = g_sum[...].astype(jnp.bfloat16).astype(jnp.float32).T[:RANK]
     ids_copy.wait()
     ids = ids_ref[...].reshape(1, tokens)
     onehot = (ids == lax.broadcasted_iota(jnp.int32, (EX_DEV, tokens), 0)).astype(jnp.float32)
@@ -157,6 +162,8 @@
             pltpu.VMEM((RANK, width), jnp.bfloat16),
             pltpu.VMEM((RANK, width), jnp.bfloat16),
             pltpu.VMEM((tokens,), jnp.int32),
+            pltpu.VMEM((tokens, 2 * RANK), jnp.float32),
+            pltpu.VMEM((tokens, 2 * RANK), jnp.float32),
             pltpu.VMEM((SLICES, 2 * EX_DEV, LANES), jnp.bfloat16),
             pltpu.VMEM((n, 2 * EX_DEV, LANES), jnp.bfloat16),
             pltpu.VMEM((SLICES, EX_DEV, examples), jnp.float32),

time: 20 us -> 19.4 us (0.970)
  Pallas kernels: 18.5 us -> 17.9 us
    pallas_call x1, Pallas kernels: 18.5 us -> 17.9 us  [shards(): pl.pallas_call(functools.partial(kernel, n), out_shape=jax.ShapeDtypeStru...]
where the time goes in v2:
time: 19.4 us; the launch traced here: 19.2 us
  Pallas kernels  17.9 us (92%)
  local copies, waits for them, and re-layouts  1.28 us (7%)
    pallas_call x1, Pallas kernels, shards(): pl.pallas_call(functools.partial(kernel, n), out_shape=jax.ShapeDtypeStru...  17.9 us
    unnamed x1, local copies, waits for them, and re-layouts  1.28 us

profile of v2, /device:TPU:0, one launch (start us, length us, event | category | flops | bytes accessed | tf_op | source)
XLA Modules:
  0.0 19.2 jit_solution(4433578804862322307)
XLA Ops:
  0.0 17.9 %shard_map.55 = f32[8,128]{1,0:T(8,128)} custom-call(bf16[256,8192]{1,0:T(8,128)(2,1)} %x_hbm.1, bf16[256,8192]{1,0:T(8,128)(2,1)} %g_hbm.1, bf16[64,8192]{1,0:T(8,128)(2,1)} %bitcast.2, bf16[64,8192]{1,0:T(8,128)(2,1)} %bitcast.3, s32[256]{0:T(256)} %ids_hbm.1), custom_call_target="tpu_custom_call" | custom-call | flops 536870912 | bytes 10485760 | tf_op jit(solution)/shard_map/pallas_call | solution.py:154
  17.9 1.3 %copy.7 = f32[8,128]{1,0:T(8,128)} copy(f32[8,128]{1,0:T(8,128)} %shard_map.55) | data formatting | bytes 8192

commit v3 on v2

--- a/solution.py
+++ b/solution.py
@@ -14,12 +14,25 @@
 LANES = 128
 SLICES = 16
 CHUNK = 1024
+NEAR = 4
 MESH = pl.DeviceIdType.MESH
 NT = (((1,), (1,)), ((), ()))
 
 
 def dot_nt(a, b):
     return lax.dot_general(a, b, NT, preferred_element_type=jnp.float32)
+
+
+def partner(me, n, i):
+    blocks = n // NEAR
+    block, place = me // NEAR, me % NEAR
+    if i >= n - NEAR:
+        return block * NEAR + (place + 1 + i - (n - NEAR)) % NEAR
+    step = i // NEAR
+    up = blocks - 1 - step
+    up = jnp.where(up <= block, up - 1, up)
+    down = jnp.where(step >= block, step + 1, step)
+    return jnp.where(2 * block < blocks, up, down) * NEAR + (place + i) % NEAR
 
 
 def kernel(
@@ -52,6 +65,12 @@
     quarter, mine = me // SLICES, me % SLICES
     chunks = x_buf.shape[1] // CHUNK
 
+    barrier = pltpu.get_barrier_semaphore()
+    for i in range(n - 1):
+        pl.semaphore_signal(
+            barrier, inc=1, device_id={"row": partner(me, n, i)}, device_id_type=MESH
+        )
+
     pairs = ((pi_hbm, pi_buf), (x_hbm, x_buf), (po_hbm, po_buf), (g_hbm, g_buf))
 
     def loads(c):
@@ -69,12 +88,6 @@
     ids_copy = pltpu.make_async_copy(ids_hbm, ids_ref, ids_sem)
     ids_copy.start()
 
-    barrier = pltpu.get_barrier_semaphore()
-    for d in range(1, n):
-        pl.semaphore_signal(
-            barrier, inc=1, device_id={"row": lax.rem(me + d, n)}, device_id_type=MESH
-        )
-
     tokens = x_buf.shape[0]
     x_sum[...] = jnp.zeros_like(x_sum)
     g_sum[...] = jnp.zeros_like(g_sum)
@@ -84,15 +97,14 @@
         cols, copies = loads(c)
         copies[0].wait()
         copies[1].wait()
-        pi = pi_buf[:, cols]
-        x_sum[...] += dot_nt(x_buf[:, cols], jnp.concatenate([pi, pi], axis=0))
+        x_sum[...] += dot_nt(x_buf[:, cols], pi_buf[:, cols])
         copies[2].wait()
         copies[3].wait()
-        po = po_buf[:, cols]
-        g_sum[...] += dot_nt(g_buf[:, cols], jnp.concatenate([po, po], axis=0))
-
-    x = x_sum[...].astype(jnp.bfloat16)
-    g = g_sum[...].astype(jnp.bfloat16).astype(jnp.float32).T[:RANK]
+        g_sum[...] += dot_nt(g_buf[:, cols], po_buf[:, cols])
+
+    x = x_sum[...]
+    x = jnp.concatenate([x, x], axis=1).astype(jnp.bfloat16)
+    g = g_sum[...].astype(jnp.bfloat16).astype(jnp.float32).T
     ids_copy.wait()
     ids = ids_ref[...].reshape(1, tokens)
     onehot = (ids == lax.broadcasted_iota(jnp.int32, (EX_DEV, tokens), 0)).astype(jnp.float32)
@@ -104,8 +116,8 @@
     feat[...] = packed.astype(jnp.bfloat16).reshape(feat.shape)
 
     pl.semaphore_wait(barrier, n - 1)
-    for d in range(1, n):
-        target = lax.rem(me + d, n)
+    for i in range(n - 1):
+        target = partner(me, n, i)
         pltpu.make_async_remote_copy(
             src_ref=feat.at[lax.rem(target, SLICES)],
             dst_ref=recv.at[me],
@@ -127,8 +139,8 @@
     own = every if n == SLICES else rows(recv[pl.ds(quarter * SLICES, SLICES)])
     gram[...] = dot_nt(own, every).reshape(gram.shape)
 
-    for d in range(1, SLICES):
-        to = lax.rem(mine + d, SLICES)
+    for i in range(SLICES - 1):
+        to = partner(mine, SLICES, i)
         pltpu.make_async_remote_copy(
             src_ref=gram.at[to],
             dst_ref=parts.at[mine],
@@ -153,7 +165,7 @@
     flops = 4 * tokens * width * RANK
     return pl.pallas_call(
         functools.partial(kernel, n),
-        out_shape=jax.ShapeDtypeStruct((EX_DEV, examples), jnp.float32),
+        out_shape=pltpu.VMEM((EX_DEV, examples), jnp.float32),
         in_specs=[hbm] * 5,
         out_specs=vmem,
         scratch_shapes=[
@@ -162,8 +174,8 @@
             pltpu.VMEM((RANK, width), jnp.bfloat16),
             pltpu.VMEM((RANK, width), jnp.bfloat16),
             pltpu.VMEM((tokens,), jnp.int32),
-            pltpu.VMEM((tokens, 2 * RANK), jnp.float32),
-            pltpu.VMEM((tokens, 2 * RANK), jnp.float32),
+            pltpu.VMEM((tokens, RANK), jnp.float32),
+            pltpu.VMEM((tokens, RANK), jnp.float32),
             pltpu.VMEM((SLICES, 2 * EX_DEV, LANES), jnp.bfloat16),
             pltpu.VMEM((n, 2 * EX_DEV, LANES), jnp.bfloat16),
             pltpu.VMEM((SLICES, EX_DEV, examples), jnp.float32),

time: 19.4 us -> 17.8 us (0.918)
  Pallas kernels: 17.9 us -> 17 us
  local copies, waits for them, and re-layouts: 1.28 us -> 0.6 us
    pallas_call x1, Pallas kernels: 17.9 us -> 17 us  [shards(): pl.pallas_call(functools.partial(kernel, n), out_shape=pltpu.VMEM((EX_DEV...]
    unnamed x1, local copies, waits for them, and re-layouts: 1.28 us -> 0.6 us
where the time goes in v3:
time: 17.8 us; the launch traced here: 17.6 us
  Pallas kernels  17 us (96%)
  local copies, waits for them, and re-layouts  0.6 us (3%)
    pallas_call x1, Pallas kernels, shards(): pl.pallas_call(functools.partial(kernel, n), out_shape=pltpu.VMEM((EX_DEV...  17 us
    unnamed x1, local copies, waits for them, and re-layouts  0.6 us

profile of v3, /device:TPU:0, one launch (start us, length us, event | category | flops | bytes accessed | tf_op | source)
XLA Modules:
  0.0 17.6 jit_solution(2198865012144852409)
XLA Ops:
  0.0 17.0 %shard_map.55 = f32[8,128]{1,0:T(8,128)S(1)} custom-call(bf16[256,8192]{1,0:T(8,128)(2,1)} %x_hbm.1, bf16[256,8192]{1,0:T(8,128)(2,1)} %g_hbm.1, bf16[64,8192]{1,0:T(8,128)(2,1)} %bitcast.2, bf16[64,8192]{1,0:T(8,128)(2,1)} %bitcast.3, s32[256]{0:T(256)} %ids_hbm.1), custom_call_target="tpu_custom_call" | custom-call | flops 536870912 | bytes 10485760 | tf_op jit(solution)/shard_map/pallas_call | solution.py:166
  17.0 0.6 %copy.7 = f32[8,128]{1,0:T(8,128)} copy(f32[8,128]{1,0:T(8,128)S(1)} %shard_map.55) | data formatting | bytes 8192

commit v4 on v3

--- a/solution.py
+++ b/solution.py
@@ -50,11 +50,13 @@
     ids_ref,
     x_sum,
     g_sum,
+    weighted,
     feat,
     recv,
     gram,
     parts,
     load_sem,
+    factor_sem,
     ids_sem,
     send_a,
     recv_a,
@@ -71,45 +73,48 @@
             barrier, inc=1, device_id={"row": partner(me, n, i)}, device_id_type=MESH
         )
 
-    pairs = ((pi_hbm, pi_buf), (x_hbm, x_buf), (po_hbm, po_buf), (g_hbm, g_buf))
-
-    def loads(c):
+    def load(src, dst, side, c):
         cols = pl.ds(pl.multiple_of(c * CHUNK, CHUNK), CHUNK)
-        return cols, [
-            pltpu.make_async_copy(src.at[:, cols], dst.at[:, cols], load_sem.at[c, i])
-            for i, (src, dst) in enumerate(pairs)
-        ]
-
-    @pl.loop(0, chunks)
-    def _(c):
-        for copy in loads(c)[1]:
-            copy.start()
-
+        return cols, pltpu.make_async_copy(src.at[:, cols], dst.at[:, cols], load_sem.at[side, c])
+
+    factors = [
+        pltpu.make_async_copy(po_hbm, po_buf, factor_sem.at[0]),
+        pltpu.make_async_copy(pi_hbm, pi_buf, factor_sem.at[1]),
+    ]
     ids_copy = pltpu.make_async_copy(ids_hbm, ids_ref, ids_sem)
     ids_copy.start()
+    streams = ((g_hbm, g_buf, 0), (x_hbm, x_buf, 1))
+    for factor, stream in zip(factors, streams):
+        factor.start()
+
+        @pl.loop(0, chunks)
+        def _(c):
+            load(*stream, c)[1].start()
+
+    def project(factor, stream, factor_buf, total):
+        total[...] = jnp.zeros_like(total)
+        factor.wait()
+
+        @pl.loop(0, chunks)
+        def _(c):
+            cols, copy = load(*stream, c)
+            copy.wait()
+            total[...] += dot_nt(stream[1][:, cols], factor_buf[:, cols])
+
+        return total[...]
 
     tokens = x_buf.shape[0]
-    x_sum[...] = jnp.zeros_like(x_sum)
-    g_sum[...] = jnp.zeros_like(g_sum)
-
-    @pl.loop(0, chunks)
-    def _(c):
-        cols, copies = loads(c)
-        copies[0].wait()
-        copies[1].wait()
-        x_sum[...] += dot_nt(x_buf[:, cols], pi_buf[:, cols])
-        copies[2].wait()
-        copies[3].wait()
-        g_sum[...] += dot_nt(g_buf[:, cols], po_buf[:, cols])
-
-    x = x_sum[...]
-    x = jnp.concatenate([x, x], axis=1).astype(jnp.bfloat16)
-    g = g_sum[...].astype(jnp.bfloat16).astype(jnp.float32).T
+    g = project(factors[0], streams[0], po_buf, g_sum)
+    g = g.astype(jnp.bfloat16).astype(jnp.float32).T
     ids_copy.wait()
     ids = ids_ref[...].reshape(1, tokens)
     onehot = (ids == lax.broadcasted_iota(jnp.int32, (EX_DEV, tokens), 0)).astype(jnp.float32)
-    weighted = (g[:, None, :] * onehot[None, :, :]).reshape(RANK * EX_DEV, tokens)
-    outer = jnp.dot(weighted.astype(jnp.bfloat16), x, preferred_element_type=jnp.float32)
+    masked = (g[:, None, :] * onehot[None, :, :]).reshape(RANK * EX_DEV, tokens)
+    weighted[...] = masked.astype(jnp.bfloat16)
+
+    x = project(factors[1], streams[1], pi_buf, x_sum)
+    x = jnp.concatenate([x, x], axis=1).astype(jnp.bfloat16)
+    outer = jnp.dot(weighted[...], x, preferred_element_type=jnp.float32)
     half = RANK * EX_DEV // 2
     low = lax.broadcasted_iota(jnp.int32, (half, LANES), 1) < RANK
     packed = jnp.where(low, outer[:half], outer[half:]) * (1.0 / math.sqrt(TPE))
@@ -176,11 +181,13 @@
             pltpu.VMEM((tokens,), jnp.int32),
             pltpu.VMEM((tokens, RANK), jnp.float32),
             pltpu.VMEM((tokens, RANK), jnp.float32),
+            pltpu.VMEM((RANK * EX_DEV, tokens), jnp.bfloat16),
             pltpu.VMEM((SLICES, 2 * EX_DEV, LANES), jnp.bfloat16),
             pltpu.VMEM((n, 2 * EX_DEV, LANES), jnp.bfloat16),
             pltpu.VMEM((SLICES, EX_DEV, examples), jnp.float32),
             pltpu.VMEM((SLICES, EX_DEV, examples), jnp.float32),
-            pltpu.SemaphoreType.DMA((width // CHUNK, 4)),
+            pltpu.SemaphoreType.DMA((2, width // CHUNK)),
+            pltpu.SemaphoreType.DMA((2,)),
             pltpu.SemaphoreType.DMA,
             pltpu.SemaphoreType.DMA,
             pltpu.SemaphoreType.DMA,

time: 17.8 us -> 18 us (1.011)
  Pallas kernels: 17 us -> 17.2 us
    pallas_call x1, Pallas kernels: 17 us -> 17.2 us  [shards(): pl.pallas_call(functools.partial(kernel, n), out_shape=pltpu.VMEM((EX_DEV...]
where the time goes in v4:
time: 18 us; the launch traced here: 17.8 us
  Pallas kernels  17.2 us (96%)
  local copies, waits for them, and re-layouts  0.6 us (3%)
    pallas_call x1, Pallas kernels, shards(): pl.pallas_call(functools.partial(kernel, n), out_shape=pltpu.VMEM((EX_DEV...  17.2 us
    unnamed x1, local copies, waits for them, and re-layouts  0.6 us

profile of v4, /device:TPU:0, one launch (start us, length us, event | category | flops | bytes accessed | tf_op | source)
XLA Modules:
  0.0 17.8 jit_solution(16315194976163567091)
XLA Ops:
  0.0 17.2 %shard_map.55 = f32[8,128]{1,0:T(8,128)S(1)} custom-call(bf16[256,8192]{1,0:T(8,128)(2,1)} %x_hbm.1, bf16[256,8192]{1,0:T(8,128)(2,1)} %g_hbm.1, bf16[64,8192]{1,0:T(8,128)(2,1)} %bitcast.2, bf16[64,8192]{1,0:T(8,128)(2,1)} %bitcast.3, s32[256]{0:T(256)} %ids_hbm.1), custom_call_target="tpu_custom_call" | custom-call | flops 536870912 | bytes 10485760 | tf_op jit(solution)/shard_map/pallas_call | solution.py:171
  17.3 0.6 %copy.7 = f32[8,128]{1,0:T(8,128)} copy(f32[8,128]{1,0:T(8,128)S(1)} %shard_map.55) | data formatting | bytes 8192

commit v5 on v4

--- a/solution.py
+++ b/solution.py
@@ -99,13 +99,13 @@
         def _(c):
             cols, copy = load(*stream, c)
             copy.wait()
-            total[...] += dot_nt(stream[1][:, cols], factor_buf[:, cols])
+            total[...] += dot_nt(factor_buf[:, cols], stream[1][:, cols])
 
         return total[...]
 
     tokens = x_buf.shape[0]
     g = project(factors[0], streams[0], po_buf, g_sum)
-    g = g.astype(jnp.bfloat16).astype(jnp.float32).T
+    g = g.astype(jnp.bfloat16).astype(jnp.float32)
     ids_copy.wait()
     ids = ids_ref[...].reshape(1, tokens)
     onehot = (ids == lax.broadcasted_iota(jnp.int32, (EX_DEV, tokens), 0)).astype(jnp.float32)
@@ -113,8 +113,7 @@
     weighted[...] = masked.astype(jnp.bfloat16)
 
     x = project(factors[1], streams[1], pi_buf, x_sum)
-    x = jnp.concatenate([x, x], axis=1).astype(jnp.bfloat16)
-    outer = jnp.dot(weighted[...], x, preferred_element_type=jnp.float32)
+    outer = dot_nt(weighted[...], jnp.concatenate([x, x], axis=0).astype(jnp.bfloat16))
     half = RANK * EX_DEV // 2
     low = lax.broadcasted_iota(jnp.int32, (half, LANES), 1) < RANK
     packed = jnp.where(low, outer[:half], outer[half:]) * (1.0 / math.sqrt(TPE))
@@ -179,8 +178,8 @@
             pltpu.VMEM((RANK, width), jnp.bfloat16),
             pltpu.VMEM((RANK, width), jnp.bfloat16),
             pltpu.VMEM((tokens,), jnp.int32),
-            pltpu.VMEM((tokens, RANK), jnp.float32),
-            pltpu.VMEM((tokens, RANK), jnp.float32),
+            pltpu.VMEM((RANK, tokens), jnp.float32),
+            pltpu.VMEM((RANK, tokens), jnp.float32),
             pltpu.VMEM((RANK * EX_DEV, tokens), jnp.bfloat16),
             pltpu.VMEM((SLICES, 2 * EX_DEV, LANES), jnp.bfloat16),
             pltpu.VMEM((n, 2 * EX_DEV, LANES), jnp.bfloat16),

time: 18 us -> 17.9 us (level)
  no operation moved by 1% of the time
where the time goes in v5:
time: 17.9 us; the launch traced here: 17.7 us
  Pallas kernels  17.1 us (96%)
  local copies, waits for them, and re-layouts  0.6 us (3%)
    pallas_call x1, Pallas kernels, shards(): pl.pallas_call(functools.partial(kernel, n), out_shape=pltpu.VMEM((EX_DEV...  17.1 us
    unnamed x1, local copies, waits for them, and re-layouts  0.6 us

profile of v5, /device:TPU:0, one launch (start us, length us, event | category | flops | bytes accessed | tf_op | source)
XLA Modules:
  0.0 17.7 jit_solution(13962384469258626005)
XLA Ops:
  0.0 17.1 %shard_map.55 = f32[8,128]{1,0:T(8,128)S(1)} custom-call(bf16[256,8192]{1,0:T(8,128)(2,1)} %x_hbm.1, bf16[256,8192]{1,0:T(8,128)(2,1)} %g_hbm.1, bf16[64,8192]{1,0:T(8,128)(2,1)} %bitcast.2, bf16[64,8192]{1,0:T(8,128)(2,1)} %bitcast.3, s32[256]{0:T(256)} %ids_hbm.1), custom_call_target="tpu_custom_call" | custom-call | flops 536870912 | bytes 10485760 | tf_op jit(solution)/shard_map/pallas_call | solution.py:170
  17.1 0.6 %copy.7 = f32[8,128]{1,0:T(8,128)} copy(f32[8,128]{1,0:T(8,128)S(1)} %shard_map.55) | data formatting | bytes 8192

commit v6 on v3

--- a/solution.py
+++ b/solution.py
@@ -71,7 +71,9 @@
             barrier, inc=1, device_id={"row": partner(me, n, i)}, device_id_type=MESH
         )
 
-    pairs = ((pi_hbm, pi_buf), (x_hbm, x_buf), (po_hbm, po_buf), (g_hbm, g_buf))
+    ids_copy = pltpu.make_async_copy(ids_hbm, ids_ref, ids_sem)
+    ids_copy.start()
+    pairs = ((po_hbm, po_buf), (g_hbm, g_buf), (pi_hbm, pi_buf), (x_hbm, x_buf))
 
     def loads(c):
         cols = pl.ds(pl.multiple_of(c * CHUNK, CHUNK), CHUNK)
@@ -85,31 +87,29 @@
         for copy in loads(c)[1]:
             copy.start()
 
-    ids_copy = pltpu.make_async_copy(ids_hbm, ids_ref, ids_sem)
-    ids_copy.start()
-
-    tokens = x_buf.shape[0]
+    g_sum[...] = jnp.zeros_like(g_sum)
     x_sum[...] = jnp.zeros_like(x_sum)
-    g_sum[...] = jnp.zeros_like(g_sum)
 
     @pl.loop(0, chunks)
     def _(c):
         cols, copies = loads(c)
-        copies[0].wait()
-        copies[1].wait()
-        x_sum[...] += dot_nt(x_buf[:, cols], pi_buf[:, cols])
-        copies[2].wait()
-        copies[3].wait()
-        g_sum[...] += dot_nt(g_buf[:, cols], po_buf[:, cols])
-
-    x = x_sum[...]
-    x = jnp.concatenate([x, x], axis=1).astype(jnp.bfloat16)
-    g = g_sum[...].astype(jnp.bfloat16).astype(jnp.float32).T
+        for copy in copies:
+            copy.wait()
+        g = dot_nt(po_buf[:, cols], g_buf[:, cols])
+        x = dot_nt(pi_buf[:, cols], x_buf[:, cols])
+        g_sum[...] += g
+        x_sum[...] += x
+
+    tokens = x_buf.shape[0]
+    g = g_sum[...].astype(jnp.bfloat16).astype(jnp.float32)
     ids_copy.wait()
     ids = ids_ref[...].reshape(1, tokens)
     onehot = (ids == lax.broadcasted_iota(jnp.int32, (EX_DEV, tokens), 0)).astype(jnp.float32)
-    weighted = (g[:, None, :] * onehot[None, :, :]).reshape(RANK * EX_DEV, tokens)
-    outer = jnp.dot(weighted.astype(jnp.bfloat16), x, preferred_element_type=jnp.float32)
+    masked = (g[:, None, :] * onehot[None, :, :]).reshape(RANK * EX_DEV, tokens)
+    weighted = masked.astype(jnp.bfloat16)
+
+    x = x_sum[...]
+    outer = dot_nt(weighted, jnp.concatenate([x, x], axis=0).astype(jnp.bfloat16))
     half = RANK * EX_DEV // 2
     low = lax.broadcasted_iota(jnp.int32, (half, LANES), 1) < RANK
     packed = jnp.where(low, outer[:half], outer[half:]) * (1.0 / math.sqrt(TPE))
@@ -174,8 +174,8 @@
             pltpu.VMEM((RANK, width), jnp.bfloat16),
             pltpu.VMEM((RANK, width), jnp.bfloat16),
             pltpu.VMEM((tokens,), jnp.int32),
-            pltpu.VMEM((tokens, RANK), jnp.float32),
-            pltpu.VMEM((tokens, RANK), jnp.float32),
+            pltpu.VMEM((RANK, tokens), jnp.float32),
+            pltpu.VMEM((RANK, tokens), jnp.float32),
             pltpu.VMEM((SLICES, 2 * EX_DEV, LANES), jnp.bfloat16),
             pltpu.VMEM((n, 2 * EX_DEV, LANES), jnp.bfloat16),
             pltpu.VMEM((SLICES, EX_DEV, examples), jnp.float32),

time: 17.8 us -> 16.9 us (0.949)
  Pallas kernels: 17 us -> 16.1 us
    pallas_call x1, Pallas kernels: 17 us -> 16.1 us  [shards(): pl.pallas_call(functools.partial(kernel, n), out_shape=pltpu.VMEM((EX_DEV...]
where the time goes in v6:
time: 16.9 us; the launch traced here: 16.7 us
  Pallas kernels  16.1 us (95%)
  local copies, waits for them, and re-layouts  0.6 us (4%)
    pallas_call x1, Pallas kernels, shards(): pl.pallas_call(functools.partial(kernel, n), out_shape=pltpu.VMEM((EX_DEV...  16.1 us
    unnamed x1, local copies, waits for them, and re-layouts  0.6 us

profile of v6, /device:TPU:0, one launch (start us, length us, event | category | flops | bytes accessed | tf_op | source)
XLA Modules:
  0.0 16.7 jit_solution(3160187267277514931)
XLA Ops:
  0.0 16.1 %shard_map.55 = f32[8,128]{1,0:T(8,128)S(1)} custom-call(bf16[256,8192]{1,0:T(8,128)(2,1)} %x_hbm.1, bf16[256,8192]{1,0:T(8,128)(2,1)} %g_hbm.1, bf16[64,8192]{1,0:T(8,128)(2,1)} %bitcast.2, bf16[64,8192]{1,0:T(8,128)(2,1)} %bitcast.3, s32[256]{0:T(256)} %ids_hbm.1), custom_call_target="tpu_custom_call" | custom-call | flops 536870912 | bytes 10485760 | tf_op jit(solution)/shard_map/pallas_call | solution.py:166
  16.1 0.6 %copy.7 = f32[8,128]{1,0:T(8,128)} copy(f32[8,128]{1,0:T(8,128)S(1)} %shard_map.55) | data formatting | bytes 8192

commit v7 on v6

--- a/solution.py
+++ b/solution.py
@@ -96,7 +96,7 @@
         for copy in copies:
             copy.wait()
         g = dot_nt(po_buf[:, cols], g_buf[:, cols])
-        x = dot_nt(pi_buf[:, cols], x_buf[:, cols])
+        x = dot_nt(x_buf[:, cols], pi_buf[:, cols])
         g_sum[...] += g
         x_sum[...] += x
 
@@ -109,7 +109,8 @@
     weighted = masked.astype(jnp.bfloat16)
 
     x = x_sum[...]
-    outer = dot_nt(weighted, jnp.concatenate([x, x], axis=0).astype(jnp.bfloat16))
+    x = jnp.concatenate([x, x], axis=1).astype(jnp.bfloat16)
+    outer = jnp.dot(weighted, x, preferred_element_type=jnp.float32)
     half = RANK * EX_DEV // 2
     low = lax.broadcasted_iota(jnp.int32, (half, LANES), 1) < RANK
     packed = jnp.where(low, outer[:half], outer[half:]) * (1.0 / math.sqrt(TPE))
@@ -174,7 +175,7 @@
             pltpu.VMEM((RANK, width), jnp.bfloat16),
             pltpu.VMEM((RANK, width), jnp.bfloat16),
             pltpu.VMEM((tokens,), jnp.int32),
-            pltpu.VMEM((RANK, tokens), jnp.float32),
+            pltpu.VMEM((tokens, RANK), jnp.float32),
             pltpu.VMEM((RANK, tokens), jnp.float32),
             pltpu.VMEM((SLICES, 2 * EX_DEV, LANES), jnp.bfloat16),
             pltpu.VMEM((n, 2 * EX_DEV, LANES), jnp.bfloat16),

time: 16.9 us -> 16.7 us (0.988)
  no operation moved by 1% of the time
where the time goes in v7:
time: 16.7 us; the launch traced here: 16.6 us
  Pallas kernels  16 us (96%)
  local copies, waits for them, and re-layouts  0.6 us (4%)
    pallas_call x1, Pallas kernels, shards(): pl.pallas_call(functools.partial(kernel, n), out_shape=pltpu.VMEM((EX_DEV...  16 us
    unnamed x1, local copies, waits for them, and re-layouts  0.6 us

profile of v7, /device:TPU:0, one launch (start us, length us, event | category | flops | bytes accessed | tf_op | source)
XLA Modules:
  0.0 16.6 jit_solution(7512947379406750488)
XLA Ops:
  0.0 16.0 %shard_map.55 = f32[8,128]{1,0:T(8,128)S(1)} custom-call(bf16[256,8192]{1,0:T(8,128)(2,1)} %x_hbm.1, bf16[256,8192]{1,0:T(8,128)(2,1)} %g_hbm.1, bf16[64,8192]{1,0:T(8,128)(2,1)} %bitcast.2, bf16[64,8192]{1,0:T(8,128)(2,1)} %bitcast.3, s32[256]{0:T(256)} %ids_hbm.1), custom_call_target="tpu_custom_call" | custom-call | flops 536870912 | bytes 10485760 | tf_op jit(solution)/shard_map/pallas_call | solution.py:167
  16.0 0.6 %copy.7 = f32[8,128]{1,0:T(8,128)} copy(f32[8,128]{1,0:T(8,128)S(1)} %shard_map.55) | data formatting | bytes 8192

commit v8 on v7

--- a/solution.py
+++ b/solution.py
@@ -14,7 +14,6 @@
 LANES = 128
 SLICES = 16
 CHUNK = 1024
-NEAR = 4
 MESH = pl.DeviceIdType.MESH
 NT = (((1,), (1,)), ((), ()))
 
@@ -24,15 +23,8 @@
 
 
 def partner(me, n, i):
-    blocks = n // NEAR
-    block, place = me // NEAR, me % NEAR
-    if i >= n - NEAR:
-        return block * NEAR + (place + 1 + i - (n - NEAR)) % NEAR
-    step = i // NEAR
-    up = blocks - 1 - step
-    up = jnp.where(up <= block, up - 1, up)
-    down = jnp.where(step >= block, step + 1, step)
-    return jnp.where(2 * block < blocks, up, down) * NEAR + (place + i) % NEAR
+    step = jnp.where(2 * me < n, 1, -1)
+    return lax.rem(me + n + step * (n - 1 - i), n)
 
 
 def kernel(
@@ -65,12 +57,6 @@
     quarter, mine = me // SLICES, me % SLICES
     chunks = x_buf.shape[1] // CHUNK
 
-    barrier = pltpu.get_barrier_semaphore()
-    for i in range(n - 1):
-        pl.semaphore_signal(
-            barrier, inc=1, device_id={"row": partner(me, n, i)}, device_id_type=MESH
-        )
-
     ids_copy = pltpu.make_async_copy(ids_hbm, ids_ref, ids_sem)
     ids_copy.start()
     pairs = ((po_hbm, po_buf), (g_hbm, g_buf), (pi_hbm, pi_buf), (x_hbm, x_buf))
@@ -82,33 +68,53 @@
             for i, (src, dst) in enumerate(pairs)
         ]
 
-    @pl.loop(0, chunks)
+    for copy in loads(0)[1]:
+        copy.start()
+
+    barrier = pltpu.get_barrier_semaphore()
+    for i in range(n - 1):
+        pl.semaphore_signal(
+            barrier, inc=1, device_id={"row": partner(me, n, i)}, device_id_type=MESH
+        )
+
+    @pl.loop(1, chunks)
     def _(c):
         for copy in loads(c)[1]:
             copy.start()
 
-    g_sum[...] = jnp.zeros_like(g_sum)
+    def project_g(c):
+        cols, copies = loads(c)
+        copies[0].wait()
+        copies[1].wait()
+        return lambda: dot_nt(po_buf[:, cols], g_buf[:, cols])
+
+    def project_x(c):
+        cols, copies = loads(c)
+        copies[2].wait()
+        copies[3].wait()
+        return lambda: dot_nt(x_buf[:, cols], pi_buf[:, cols])
+
+    g_sum[...] = project_g(0)()
     x_sum[...] = jnp.zeros_like(x_sum)
 
-    @pl.loop(0, chunks)
+    @pl.loop(1, chunks)
     def _(c):
-        cols, copies = loads(c)
-        for copy in copies:
-            copy.wait()
-        g = dot_nt(po_buf[:, cols], g_buf[:, cols])
-        x = dot_nt(x_buf[:, cols], pi_buf[:, cols])
+        x_part = project_x(c - 1)
+        g_part = project_g(c)
+        g, x = g_part(), x_part()
         g_sum[...] += g
         x_sum[...] += x
 
+    ids_copy.wait()
+    x = x_sum[...] + project_x(chunks - 1)()
+
     tokens = x_buf.shape[0]
     g = g_sum[...].astype(jnp.bfloat16).astype(jnp.float32)
-    ids_copy.wait()
     ids = ids_ref[...].reshape(1, tokens)
     onehot = (ids == lax.broadcasted_iota(jnp.int32, (EX_DEV, tokens), 0)).astype(jnp.float32)
     masked = (g[:, None, :] * onehot[None, :, :]).reshape(RANK * EX_DEV, tokens)
     weighted = masked.astype(jnp.bfloat16)
 
-    x = x_sum[...]
     x = jnp.concatenate([x, x], axis=1).astype(jnp.bfloat16)
     outer = jnp.dot(weighted, x, preferred_element_type=jnp.float32)
     half = RANK * EX_DEV // 2

time: 16.7 us -> 16.8 us (level)
  no operation moved by 1% of the time
where the time goes in v8:
time: 16.8 us; the launch traced here: 16.6 us
  Pallas kernels  16 us (95%)
  local copies, waits for them, and re-layouts  0.6 us (4%)
    pallas_call x1, Pallas kernels, shards(): pl.pallas_call(functools.partial(kernel, n), out_shape=pltpu.VMEM((EX_DEV...  16 us
    unnamed x1, local copies, waits for them, and re-layouts  0.6 us

profile of v8, /device:TPU:0, one launch (start us, length us, event | category | flops | bytes accessed | tf_op | source)
XLA Modules:
  0.0 16.6 jit_solution(10628646833973045543)
XLA Ops:
  0.0 16.0 %shard_map.55 = f32[8,128]{1,0:T(8,128)S(1)} custom-call(bf16[256,8192]{1,0:T(8,128)(2,1)} %x_hbm.1, bf16[256,8192]{1,0:T(8,128)(2,1)} %g_hbm.1, bf16[64,8192]{1,0:T(8,128)(2,1)} %bitcast.2, bf16[64,8192]{1,0:T(8,128)(2,1)} %bitcast.3, s32[256]{0:T(256)} %ids_hbm.1), custom_call_target="tpu_custom_call" | custom-call | flops 536870912 | bytes 10485760 | tf_op jit(solution)/shard_map/pallas_call | solution.py:173
  16.0 0.6 %copy.7 = f32[8,128]{1,0:T(8,128)} copy(f32[8,128]{1,0:T(8,128)S(1)} %shard_map.55) | data formatting | bytes 8192

commit v9 on v8

--- a/solution.py
+++ b/solution.py
@@ -72,7 +72,8 @@
         copy.start()
 
     barrier = pltpu.get_barrier_semaphore()
-    for i in range(n - 1):
+    @pl.loop(0, n - 1)
+    def _(i):
         pl.semaphore_signal(
             barrier, inc=1, device_id={"row": partner(me, n, i)}, device_id_type=MESH
         )
@@ -123,7 +124,8 @@
     feat[...] = packed.astype(jnp.bfloat16).reshape(feat.shape)
 
     pl.semaphore_wait(barrier, n - 1)
-    for i in range(n - 1):
+    @pl.loop(0, n - 1)
+    def _(i):
         target = partner(me, n, i)
         pltpu.make_async_remote_copy(
             src_ref=feat.at[lax.rem(target, SLICES)],
@@ -133,6 +135,7 @@
             device_id={"row": target},
             device_id_type=MESH,
         ).start()
+
     recv[me] = feat[mine]
     rest = recv.at[pl.ds(0, n - 1)]
     pltpu.make_async_copy(rest, rest, recv_a).wait()
@@ -146,7 +149,8 @@
     own = every if n == SLICES else rows(recv[pl.ds(quarter * SLICES, SLICES)])
     gram[...] = dot_nt(own, every).reshape(gram.shape)
 
-    for i in range(SLICES - 1):
+    @pl.loop(0, SLICES - 1)
+    def _(i):
         to = partner(mine, SLICES, i)
         pltpu.make_async_remote_copy(
             src_ref=gram.at[to],
@@ -156,6 +160,7 @@
             device_id={"row": quarter * SLICES + to},
             device_id_type=MESH,
         ).start()
+
     parts[mine] = gram[mine]
     rest_b = parts.at[pl.ds(0, SLICES - 1)]
     pltpu.make_async_copy(rest_b, rest_b, recv_b).wait()

time: 16.8 us -> 16.9 us (level)
  no operation moved by 1% of the time
where the time goes in v9:
time: 16.9 us; the launch traced here: 16.7 us
  Pallas kernels  16.1 us (95%)
  local copies, waits for them, and re-layouts  0.6 us (4%)
    pallas_call x1, Pallas kernels, shards(): pl.pallas_call(functools.partial(kernel, n), out_shape=pltpu.VMEM((EX_DEV...  16.1 us
    unnamed x1, local copies, waits for them, and re-layouts  0.6 us

profile of v9, /device:TPU:0, one launch (start us, length us, event | category | flops | bytes accessed | tf_op | source)
XLA Modules:
  0.0 16.7 jit_solution(3142985978203348693)
XLA Ops:
  0.0 16.1 %shard_map.55 = f32[8,128]{1,0:T(8,128)S(1)} custom-call(bf16[256,8192]{1,0:T(8,128)(2,1)} %x_hbm.1, bf16[256,8192]{1,0:T(8,128)(2,1)} %g_hbm.1, bf16[64,8192]{1,0:T(8,128)(2,1)} %bitcast.2, bf16[64,8192]{1,0:T(8,128)(2,1)} %bitcast.3, s32[256]{0:T(256)} %ids_hbm.1), custom_call_target="tpu_custom_call" | custom-call | flops 536870912 | bytes 10485760 | tf_op jit(solution)/shard_map/pallas_call | solution.py:178
  16.1 0.6 %copy.7 = f32[8,128]{1,0:T(8,128)} copy(f32[8,128]{1,0:T(8,128)S(1)} %shard_map.55) | data formatting | bytes 8192

commit v10 on v8

--- a/solution.py
+++ b/solution.py
@@ -14,6 +14,8 @@
 LANES = 128
 SLICES = 16
 CHUNK = 1024
+NEAR = 4
+PAIR = 2
 MESH = pl.DeviceIdType.MESH
 NT = (((1,), (1,)), ((), ()))
 
@@ -23,8 +25,15 @@
 
 
 def partner(me, n, i):
-    step = jnp.where(2 * me < n, 1, -1)
-    return lax.rem(me + n + step * (n - 1 - i), n)
+    blocks = n // NEAR
+    block, place = lax.div(me, NEAR), lax.rem(me, NEAR)
+    if i >= n - NEAR:
+        return block * NEAR + lax.rem(place + 1 + i - (n - NEAR), NEAR)
+    step = i // NEAR
+    up = blocks - 1 - step
+    up = jnp.where(up <= block, up - 1, up)
+    down = jnp.where(step >= block, step + 1, step)
+    return jnp.where(2 * block < blocks, up, down) * NEAR + lax.rem(place + i, NEAR)
 
 
 def kernel(
@@ -45,11 +54,14 @@
     feat,
     recv,
     gram,
+    swapped,
+    sums,
     parts,
     load_sem,
     ids_sem,
     send_a,
     recv_a,
+    swap_sem,
     send_b,
     recv_b,
 ):
@@ -133,6 +145,7 @@
             device_id={"row": target},
             device_id_type=MESH,
         ).start()
+
     recv[me] = feat[mine]
     rest = recv.at[pl.ds(0, n - 1)]
     pltpu.make_async_copy(rest, rest, recv_a).wait()
@@ -144,22 +157,39 @@
 
     every = rows(recv[...])
     own = every if n == SLICES else rows(recv[pl.ds(quarter * SLICES, SLICES)])
-    gram[...] = dot_nt(own, every).reshape(gram.shape)
-
-    for i in range(SLICES - 1):
-        to = partner(mine, SLICES, i)
+    products = dot_nt(own, every).reshape(-1, PAIR, EX_DEV, every.shape[0])
+    for core in range(PAIR):
+        gram[core] = products[:, core]
+
+    chips = SLICES // PAIR
+    chip, side = lax.div(mine, PAIR), lax.rem(mine, PAIR)
+    swap = pltpu.make_async_remote_copy(
+        src_ref=gram.at[1 - side],
+        dst_ref=swapped,
+        send_sem=swap_sem.at[0],
+        recv_sem=swap_sem.at[1],
+        device_id={"row": me + 1 - 2 * side},
+        device_id_type=MESH,
+    )
+    swap.start()
+    swap.wait_recv()
+    sums[...] = gram[side] + swapped[...]
+
+    for i in range(chips - 1):
+        to = partner(chip, chips, i)
         pltpu.make_async_remote_copy(
-            src_ref=gram.at[to],
-            dst_ref=parts.at[mine],
+            src_ref=sums.at[to],
+            dst_ref=parts.at[chip],
             send_sem=send_b,
             recv_sem=recv_b,
-            device_id={"row": quarter * SLICES + to},
+            device_id={"row": quarter * SLICES + to * PAIR + side},
             device_id_type=MESH,
         ).start()
-    parts[mine] = gram[mine]
-    rest_b = parts.at[pl.ds(0, SLICES - 1)]
+    parts[chip] = sums[chip]
+    rest_b = parts.at[pl.ds(0, chips - 1)]
     pltpu.make_async_copy(rest_b, rest_b, recv_b).wait()
     out_ref[...] = jnp.sum(parts[...], axis=0) * (1.0 / RANK)
+    swap.wait_send()
     pltpu.make_async_copy(rest, rest, send_a).wait()
     pltpu.make_async_copy(rest_b, rest_b, send_b).wait()
 
@@ -185,12 +215,15 @@
             pltpu.VMEM((RANK, tokens), jnp.float32),
             pltpu.VMEM((SLICES, 2 * EX_DEV, LANES), jnp.bfloat16),
             pltpu.VMEM((n, 2 * EX_DEV, LANES), jnp.bfloat16),
-            pltpu.VMEM((SLICES, EX_DEV, examples), jnp.float32),
-            pltpu.VMEM((SLICES, EX_DEV, examples), jnp.float32),
+            pltpu.VMEM((PAIR, SLICES // PAIR, EX_DEV, examples), jnp.float32),
+            pltpu.VMEM((SLICES // PAIR, EX_DEV, examples), jnp.float32),
+            pltpu.VMEM((SLICES // PAIR, EX_DEV, examples), jnp.float32),
+            pltpu.VMEM((SLICES // PAIR, EX_DEV, examples), jnp.float32),
             pltpu.SemaphoreType.DMA((width // CHUNK, 4)),
             pltpu.SemaphoreType.DMA,
             pltpu.SemaphoreType.DMA,
             pltpu.SemaphoreType.DMA,
+            pltpu.SemaphoreType.DMA((2,)),
             pltpu.SemaphoreType.DMA,
             pltpu.SemaphoreType.DMA,
         ],

time: 16.8 us -> 17.5 us (1.042)
  Pallas kernels: 16 us -> 16.8 us
    pallas_call x1, Pallas kernels: 16 us -> 16.8 us  [shards(): pl.pallas_call(functools.partial(kernel, n), out_shape=pltpu.VMEM((EX_DEV...]
where the time goes in v10:
time: 17.5 us; the launch traced here: 17.4 us
  Pallas kernels  16.8 us (96%)
  local copies, waits for them, and re-layouts  0.6 us (3%)
    pallas_call x1, Pallas kernels, shards(): pl.pallas_call(functools.partial(kernel, n), out_shape=pltpu.VMEM((EX_DEV...  16.8 us
    unnamed x1, local copies, waits for them, and re-layouts  0.6 us

profile of v10, /device:TPU:0, one launch (start us, length us, event | category | flops | bytes accessed | tf_op | source)
XLA Modules:
  0.0 17.4 jit_solution(10717754962899637505)
XLA Ops:
  0.0 16.8 %shard_map.55 = f32[8,128]{1,0:T(8,128)S(1)} custom-call(bf16[256,8192]{1,0:T(8,128)(2,1)} %x_hbm.1, bf16[256,8192]{1,0:T(8,128)(2,1)} %g_hbm.1, bf16[64,8192]{1,0:T(8,128)(2,1)} %bitcast.2, bf16[64,8192]{1,0:T(8,128)(2,1)} %bitcast.3, s32[256]{0:T(256)} %ids_hbm.1), custom_call_target="tpu_custom_call" | custom-call | flops 536870912 | bytes 10485760 | tf_op jit(solution)/shard_map/pallas_call | solution.py:203
  16.8 0.6 %copy.7 = f32[8,128]{1,0:T(8,128)} copy(f32[8,128]{1,0:T(8,128)S(1)} %shard_map.55) | data formatting | bytes 8192

commit v11 on v7

--- a/solution.py
+++ b/solution.py
@@ -13,7 +13,7 @@
 EX_DEV = 8
 LANES = 128
 SLICES = 16
-CHUNK = 1024
+CHUNK = 2048
 NEAR = 4
 MESH = pl.DeviceIdType.MESH
 NT = (((1,), (1,)), ((), ()))
@@ -25,14 +25,14 @@
 
 def partner(me, n, i):
     blocks = n // NEAR
-    block, place = me // NEAR, me % NEAR
+    block, place = lax.div(me, NEAR), lax.rem(me, NEAR)
     if i >= n - NEAR:
-        return block * NEAR + (place + 1 + i - (n - NEAR)) % NEAR
+        return block * NEAR + lax.rem(place + 1 + i - (n - NEAR), NEAR)
     step = i // NEAR
     up = blocks - 1 - step
     up = jnp.where(up <= block, up - 1, up)
     down = jnp.where(step >= block, step + 1, step)
-    return jnp.where(2 * block < blocks, up, down) * NEAR + (place + i) % NEAR
+    return jnp.where(2 * block < blocks, up, down) * NEAR + lax.rem(place + i, NEAR)
 
 
 def kernel(
@@ -65,12 +65,6 @@
     quarter, mine = me // SLICES, me % SLICES
     chunks = x_buf.shape[1] // CHUNK
 
-    barrier = pltpu.get_barrier_semaphore()
-    for i in range(n - 1):
-        pl.semaphore_signal(
-            barrier, inc=1, device_id={"row": partner(me, n, i)}, device_id_type=MESH
-        )
-
     ids_copy = pltpu.make_async_copy(ids_hbm, ids_ref, ids_sem)
     ids_copy.start()
     pairs = ((po_hbm, po_buf), (g_hbm, g_buf), (pi_hbm, pi_buf), (x_hbm, x_buf))
@@ -82,7 +76,16 @@
             for i, (src, dst) in enumerate(pairs)
         ]
 
-    @pl.loop(0, chunks)
+    for copy in loads(0)[1]:
+        copy.start()
+
+    barrier = pltpu.get_barrier_semaphore()
+    for i in range(n - 1):
+        pl.semaphore_signal(
+            barrier, inc=1, device_id={"row": partner(me, n, i)}, device_id_type=MESH
+        )
+
+    @pl.loop(1, chunks)
     def _(c):
         for copy in loads(c)[1]:
             copy.start()

time: 16.7 us -> 16.6 us (level)
  no operation moved by 1% of the time
where the time goes in v11:
time: 16.6 us; the launch traced here: 16.5 us
  Pallas kernels  15.9 us (96%)
  local copies, waits for them, and re-layouts  0.6 us (4%)
    pallas_call x1, Pallas kernels, shards(): pl.pallas_call(functools.partial(kernel, n), out_shape=pltpu.VMEM((EX_DEV...  15.9 us
    unnamed x1, local copies, waits for them, and re-layouts  0.6 us

profile of v11, /device:TPU:0, one launch (start us, length us, event | category | flops | bytes accessed | tf_op | source)
XLA Modules:
  0.0 16.5 jit_solution(13528160401327419618)
XLA Ops:
  0.0 15.9 %shard_map.55 = f32[8,128]{1,0:T(8,128)S(1)} custom-call(bf16[256,8192]{1,0:T(8,128)(2,1)} %x_hbm.1, bf16[256,8192]{1,0:T(8,128)(2,1)} %g_hbm.1, bf16[64,8192]{1,0:T(8,128)(2,1)} %bitcast.2, bf16[64,8192]{1,0:T(8,128)(2,1)} %bitcast.3, s32[256]{0:T(256)} %ids_hbm.1), custom_call_target="tpu_custom_call" | custom-call | flops 536870912 | bytes 10485760 | tf_op jit(solution)/shard_map/pallas_call | solution.py:170
  15.9 0.6 %copy.7 = f32[8,128]{1,0:T(8,128)} copy(f32[8,128]{1,0:T(8,128)S(1)} %shard_map.55) | data formatting | bytes 8192

commit v12 on v11

--- a/solution.py
+++ b/solution.py
@@ -103,6 +103,8 @@
         g_sum[...] += g
         x_sum[...] += x
 
+    pl.semaphore_wait(barrier, n - 1)
+
     tokens = x_buf.shape[0]
     g = g_sum[...].astype(jnp.bfloat16).astype(jnp.float32)
     ids_copy.wait()
@@ -119,7 +121,6 @@
     packed = jnp.where(low, outer[:half], outer[half:]) * (1.0 / math.sqrt(TPE))
     feat[...] = packed.astype(jnp.bfloat16).reshape(feat.shape)
 
-    pl.semaphore_wait(barrier, n - 1)
     for i in range(n - 1):
         target = partner(me, n, i)
         pltpu.make_async_remote_copy(

time: 16.6 us -> 16.7 us (level)
  no operation moved by 1% of the time
where the time goes in v12:
time: 16.7 us; the launch traced here: 16.5 us
  Pallas kernels  15.9 us (95%)
  local copies, waits for them, and re-layouts  0.6 us (4%)
    pallas_call x1, Pallas kernels, shards(): pl.pallas_call(functools.partial(kernel, n), out_shape=pltpu.VMEM((EX_DEV...  15.9 us
    unnamed x1, local copies, waits for them, and re-layouts  0.6 us

profile of v12, /device:TPU:0, one launch (start us, length us, event | category | flops | bytes accessed | tf_op | source)
XLA Modules:
  0.0 16.5 jit_solution(5470286609503402528)
XLA Ops:
  0.0 15.9 %shard_map.55 = f32[8,128]{1,0:T(8,128)S(1)} custom-call(bf16[256,8192]{1,0:T(8,128)(2,1)} %x_hbm.1, bf16[256,8192]{1,0:T(8,128)(2,1)} %g_hbm.1, bf16[64,8192]{1,0:T(8,128)(2,1)} %bitcast.2, bf16[64,8192]{1,0:T(8,128)(2,1)} %bitcast.3, s32[256]{0:T(256)} %ids_hbm.1), custom_call_target="tpu_custom_call" | custom-call | flops 536870912 | bytes 10485760 | tf_op jit(solution)/shard_map/pallas_call | solution.py:171
  15.9 0.6 %copy.7 = f32[8,128]{1,0:T(8,128)} copy(f32[8,128]{1,0:T(8,128)S(1)} %shard_map.55) | data formatting | bytes 8192

commit v13 on v11

--- a/solution.py
+++ b/solution.py
@@ -76,8 +76,8 @@
             for i, (src, dst) in enumerate(pairs)
         ]
 
-    for copy in loads(0)[1]:
-        copy.start()
+    for i, copy in enumerate(loads(0)[1]):
+        copy.start(priority=i // 2)
 
     barrier = pltpu.get_barrier_semaphore()
     for i in range(n - 1):
@@ -87,8 +87,8 @@
 
     @pl.loop(1, chunks)
     def _(c):
-        for copy in loads(c)[1]:
-            copy.start()
+        for i, copy in enumerate(loads(c)[1]):
+            copy.start(priority=i // 2)
 
     g_sum[...] = jnp.zeros_like(g_sum)
     x_sum[...] = jnp.zeros_like(x_sum)

time: 16.6 us -> 17.6 us (1.060)
  Pallas kernels: 15.9 us -> 16.8 us
    pallas_call x1, Pallas kernels: 15.9 us -> 16.8 us  [shards(): pl.pallas_call(functools.partial(kernel, n), out_shape=pltpu.VMEM((EX_DEV...]
where the time goes in v13:
time: 17.6 us; the launch traced here: 17.4 us
  Pallas kernels  16.8 us (95%)
  local copies, waits for them, and re-layouts  0.6 us (3%)
    pallas_call x1, Pallas kernels, shards(): pl.pallas_call(functools.partial(kernel, n), out_shape=pltpu.VMEM((EX_DEV...  16.8 us
    unnamed x1, local copies, waits for them, and re-layouts  0.6 us

profile of v13, /device:TPU:0, one launch (start us, length us, event | category | flops | bytes accessed | tf_op | source)
XLA Modules:
  0.0 17.4 jit_solution(2650600211293971014)
XLA Ops:
  0.0 16.8 %shard_map.55 = f32[8,128]{1,0:T(8,128)S(1)} custom-call(bf16[256,8192]{1,0:T(8,128)(2,1)} %x_hbm.1, bf16[256,8192]{1,0:T(8,128)(2,1)} %g_hbm.1, bf16[64,8192]{1,0:T(8,128)(2,1)} %bitcast.2, bf16[64,8192]{1,0:T(8,128)(2,1)} %bitcast.3, s32[256]{0:T(256)} %ids_hbm.1), custom_call_target="tpu_custom_call" | custom-call | flops 536870912 | bytes 10485760 | tf_op jit(solution)/shard_map/pallas_call | solution.py:170
  16.8 0.6 %copy.7 = f32[8,128]{1,0:T(8,128)} copy(f32[8,128]{1,0:T(8,128)S(1)} %shard_map.55) | data formatting | bytes 8192
